TPU v7x, 256 devices: a whole 4x4x8 slice. The times are simulated.
256 devices in a mesh: src: 16 (over z, y_hi), space: 16 (over y_lo, x, core).
Axes of the slice: x: 4, y: 4 (y_hi: 2, y_lo: 2; y = y_hi * 2 + y_lo), z: 8, core: 2. Of those that a mesh axis runs over, the one named last changes fastest.
Arguments:
- wavefield: float32 [16, 9, 128, 64, 128], P('src', None, 'space'), may hold values from -6 to 6
- strain_bank: bfloat16 [16, 6, 128, 64, 128], P('src', None, 'space'), may hold values from -6 to 6
- owners: int32 [4], replicated, may hold values from 0 to 15, as said below
- region: int32 [128, 64, 128], P('space'), may hold values from 0 to 7
- region_lambda: float32 [8], replicated, may hold values from 1 to 2
- region_mu: float32 [8], replicated, may hold values from 0.5 to 1
- region_buoyancy: float32 [8], replicated, may hold values from 0.5 to 1
Outputs:
- new_wavefield: float32 [16, 9, 128, 64, 128], P('src', None, 'space')
- lambda_kernel: float32 [128, 64, 128], P('space', 'src')
- mu_kernel: float32 [128, 64, 128], P('space', 'src')
Inputs may be any that keep to these rules, and one draw needn't show every extreme that they name: `owners`: 4 distinct owner indices in an order drawn per run; 0 and 15 are always among them.
All inputs are finite; a program needn't handle non-finite values.
Results may differ from a plain program's by a relative error of at most 0.0003.
Values may be sent and summed in bfloat16 or wider, within the bound.
No kernel may reach another device: no remote copies, remote signals or barrier semaphores. Data moves between devices by JAX's collectives and lax.ppermute only.
A program may use at most 128 MiB of HBM per device.

v0:
```python
import jax
import jax.numpy as jnp
from jax import lax
from jax.sharding import PartitionSpec as P

STEPS = 4


step_size = 0.3
x_force_terms = (0, 5, 4)
y_force_terms = (5, 1, 3)
z_force_terms = (4, 3, 2)


def spread(block, axis, owner):
    block = jnp.where(lax.axis_index(axis) == owner, block, jnp.zeros_like(block))
    return lax.psum(block, axis)


def extended(x, sides, width):
    for axis, dim in sides:
        devices, length = (lax.axis_size(axis), x.shape[dim])
        up = [(i, (i + 1) % devices) for i in range(devices - 1)]
        down = [(j, i) for i, j in up]
        last = lax.slice_in_dim(x, length - width, length, axis=dim)
        initial = lax.slice_in_dim(x, 0, width, axis=dim)
        before = lax.ppermute(last, axis, up)
        after = lax.ppermute(initial, axis, down)
        x = jnp.concatenate([before, x, after], axis=dim)
    return x


def slab_of(values, along, start, length):
    slicer = [slice(None)] * values.ndim
    slicer[values.ndim + along] = slice(start, start + length)
    return values[tuple(slicer)]


def diff_valid(padded, along):
    length = padded.shape[along] - 4
    near = slab_of(padded, along, 3, length) - slab_of(padded, along, 1, length)
    far = slab_of(padded, along, 4, length) - slab_of(padded, along, 0, length)
    return (8.0 * near - far) / 12.0


def diff_zero(values, along):
    widths = [(0, 0)] * values.ndim
    widths[values.ndim + along] = (2, 2)
    return diff_valid(jnp.pad(values, widths), along)


def component(values, which):
    return values[..., which, :, :, :]


def pick_terms(values, order):
    return jnp.stack([component(values, which) for which in order], -4)


def stress_update(stress, grad_x, grad_y, grad_z, lame_first, shear):
    diagonal = [component(grad_x, 0), component(grad_y, 1), component(grad_z, 2)]
    divergence = diagonal[0] + diagonal[1] + diagonal[2]
    parts = [
        component(stress, which)
        + step_size * (lame_first * divergence + 2.0 * shear * diagonal[which])
        for which in range(3)
    ]
    parts.append(
        component(stress, 3) + step_size * shear * (component(grad_z, 1) + component(grad_y, 2))
    )
    parts.append(
        component(stress, 4) + step_size * shear * (component(grad_z, 0) + component(grad_x, 2))
    )
    parts.append(
        component(stress, 5) + step_size * shear * (component(grad_y, 0) + component(grad_x, 1))
    )
    return jnp.stack(parts, -4)


def correlate(stress, receiver, lame_first, shear):
    trace = component(stress, 0) + component(stress, 1) + component(stress, 2)
    theta = trace / (3.0 * lame_first + 2.0 * shear)
    recv_trace = receiver[0] + receiver[1] + receiver[2]
    term_lambda = step_size * theta * recv_trace
    inner = jnp.zeros_like(theta)
    for which in range(3):
        inner = (
            inner
            + (component(stress, which) - lame_first * theta) / (2.0 * shear) * receiver[which]
        )
    for which in range(3, 6):
        inner = inner + component(stress, which) / shear * receiver[which]
    term_mu = step_size * 2.0 * inner
    return (term_lambda, term_mu)


def material(region, region_lambda, region_mu, region_buoyancy):
    labels = jnp.arange(region_lambda.shape[0], dtype=jnp.int32)
    onehot = (region[None] == labels[:, None, None, None]).astype(jnp.float32)
    return [
        jnp.sum(onehot * table[:, None, None, None], 0)
        for table in (region_lambda, region_mu, region_buoyancy)
    ]


def local(wavefield, strain_bank, owners, region, region_lambda, region_mu, region_buoyancy):
    lame_first, shear, buoyancy = material(region, region_lambda, region_mu, region_buoyancy)
    state = wavefield
    kernel_lambda = jnp.zeros(region.shape, jnp.float32)
    kernel_mu = jnp.zeros(region.shape, jnp.float32)
    for time_step in range(STEPS):
        receiver = spread(strain_bank, "src", owners[time_step])[0].astype(jnp.float32)
        velocity = state[:, 0:3]
        stress = state[:, 3:9]
        padded = extended(stress, (("space", 2),), 2)
        force = (
            diff_valid(pick_terms(padded, x_force_terms), -3)
            + diff_zero(pick_terms(stress, y_force_terms), -2)
            + diff_zero(pick_terms(stress, z_force_terms), -1)
        )
        velocity = velocity + step_size * buoyancy * force
        grad_x = diff_valid(extended(velocity, (("space", 2),), 2), -3)
        stress = stress_update(
            stress, grad_x, diff_zero(velocity, -2), diff_zero(velocity, -1), lame_first, shear
        )
        state = jnp.concatenate([velocity, stress], -4)
        term_lambda, term_mu = correlate(stress, receiver, lame_first, shear)
        kernel_lambda = kernel_lambda + jnp.sum(term_lambda, 0)
        kernel_mu = kernel_mu + jnp.sum(term_mu, 0)
    summed = (
        lax.psum_scatter(kernel_lambda, "src", scatter_dimension=1, tiled=True),
        lax.psum_scatter(kernel_mu, "src", scatter_dimension=1, tiled=True),
    )
    return (state, summed[0], summed[1])


def solution(mesh):
    in_specs = (
        P("src", None, "space", None, None),
        P("src", None, "space", None, None),
        P(),
        P("space", None, None),
        P(),
        P(),
        P(),
    )
    out_specs = (
        P("src", None, "space", None, None),
        P("space", "src", None),
        P("space", "src", None),
    )
    return jax.shard_map(local, mesh=mesh, in_specs=in_specs, out_specs=out_specs, check_vma=False)
```

profile of v0, /device:TPU:2, one launch (start us, length us, event | category | flops | bytes accessed | tf_op | source)
XLA Modules:
  0.0 722.4 jit_solution(13448058246037452301)
XLA Ops:
  7.2 1.2 fusion.273
  8.4 2.1 collective-permute-start
  10.5 3.6 collective-permute-start.1
  14.1 1.4 fusion.274
  16.7 0.9 collective-permute-done
  17.7 1.8 collective-permute-done.1
  20.3 3.8 collective-permute-start.2
  24.1 1.9 collective-permute-start.3
  26.1 1.2 collective-permute-done.2
  27.3 3.8 collective-permute-done.3
  31.1 1.3 fusion.14
  34.0 1.9 collective-permute-start.4
  35.9 3.6 collective-permute-start.5
  40.2 2.9 collective-permute-done.4
  43.1 1.8 collective-permute-done.5
  45.7 0.9 fusion.280
  46.6 3.8 collective-permute-start.6
  50.4 1.9 collective-permute-start.7
  52.4 1.5 collective-permute-done.6
  53.9 3.8 collective-permute-done.7
  57.7 6.2 fusion.19
  64.0 2.2 constant_dynamic-update-slice_fusion.11
  68.7 0.8 constant_dynamic-update-slice_fusion.6
  69.5 1.1 copy-done.35
  70.7 0.9 fusion.276
  71.6 1.9 collective-permute-start.8
  73.5 3.6 collective-permute-start.9
  80.5 1.2 select_maximum_fusion.34
  83.1 1.4 fusion.3
  85.2 0.8 fusion.279
  86.1 3.5 collective-permute-start.10
  89.6 1.9 collective-permute-start.11
  91.5 1.7 broadcast_select_fusion
  93.5 3.3 collective-permute-done.11
  96.9 6.2 fusion.24
  103.3 1.0 copy-done.46
  106.4 1.9 collective-permute-start.12
  108.3 3.6 collective-permute-start.13
  112.6 2.9 collective-permute-done.12
  115.5 1.8 collective-permute-done.13
  117.3 1.6 constant_dynamic-update-slice_fusion.18
  118.9 3.8 collective-permute-start.14
  122.8 7.0 collective-permute-start.15
  129.7 1.0 collective-permute-done.15
  130.8 1.3 fusion.29
  132.1 0.9 copy-done.4
  133.0 0.9 fusion.247
  134.7 169.6 %all-reduce.19.cloned.1.call-done = (bf16[1,6,8,64,128]{4,3,2,1,0:T(8,128)(2,1)}, bf16[1,6,8,64,128]{4,3,2,1,0:T(8,128)(2,1)}, bf16[1,6,8,64,128]{4,3,2,1,0:T(8,128)(2,1)}, bf16[1,6,8,64,128]{4,3,2,1,0:T(8,128)(2,1)}) async-done(((bf16[1,6,8,64,128]{4,3,2,1,0:T(8,128)(2,1)}, bf16[1,6,8,64,128]{4,3,2,1,0:T(8,128)(2,1)}, bf16[1,6,8,64,128]{4,3,2,1,0:T(8,128)(2,1)}, bf16[1,6,8,64,128]{4,3,2,1,0:T(8,128)(2,1)}), ...) | async-done | bytes 3145744 | tf_op jit(solution)/shard_map/psum | solution.py:17
  304.3 1.4 convert_element_type.35
  305.8 1.9 convert_element_type.36
  307.7 1.9 convert_element_type.37
  309.7 1.9 convert_element_type.38
  312.2 2.2 fusion.123
  314.5 0.8 copy.28
  315.4 1.8 fusion.255
  317.2 3.7 add_bitcast_fusion
  320.9 0.8 copy.27
  321.8 1.8 fusion.212
  323.7 1.7 fusion.214
  325.4 1.7 fusion.216
  327.1 185.2 %reduce-scatter.5.cloned.1.call-done = f32[8,4,128]{2,0,1:T(8,128)} async-done(((f32[8,64,128]{2,0,1:T(8,128)}), f32[8,4,128]{2,0,1:T(8,128)}) %reduce-scatter.5.cloned.1.call-update) | async-done | bytes 16400 | tf_op jit(solution)/shard_map/reduce_scatter | solution.py:132
  512.3 1.3 copy.30
  513.6 200.9 %reduce-scatter.3.cloned.1.call-done = f32[8,4,128]{2,0,1:T(8,128)} async-done(((f32[8,64,128]{2,0,1:T(8,128)}), f32[8,4,128]{2,0,1:T(8,128)}) %reduce-scatter.3.cloned.1.call-update) | async-done | bytes 16400 | tf_op jit(solution)/shard_map/reduce_scatter | solution.py:131
  714.5 1.3 copy.29
  (182 shorter events, 14.8 us)
Async XLA Ops:
  7.2 297.1 %all-reduce.19.cloned.1.call-start = ((), (), s32[]{:S(2)}) async-start(), calls=%async_computation.4 | async-start | bytes 6291456 | tf_op jit(solution)/shard_map/psum | solution.py:17
  8.4 7.1 copy-start.63
  8.4 7.1 copy-start.65
  8.4 7.1 copy-start.66
  8.4 7.1 copy-start.67
  8.4 9.2 %collective-permute-start = (f32[1,6,2,64,128]{4,3,2,1,0:T(8,128)S(1)}, f32[1,6,2,64,128]{4,3,2,1,0:T(8,128)S(1)}, u32[]{:S(2)}, u32[]{:S(2)}) collective-permute-start(f32[1,6,2,64,128]{4,3,2,1,0:T(8,128)S(1)} %get-tuple-element.57), channel_id=1, source_target_pairs={{0,1},{1,2},{2,3},{3,4},{4,5},{5,6},{6,7},{7,8},{8,9},{9,10},{10,1... | collective-permute-start | bytes 1179656 | tf_op jit(solution)/shard_map/ppermute | solution.py:27
  10.5 8.9 %collective-permute-start.1 = (f32[1,6,2,64,128]{4,3,2,1,0:T(8,128)S(1)}, f32[1,6,2,64,128]{4,3,2,1,0:T(8,128)S(1)}, u32[]{:S(2)}, u32[]{:S(2)}) collective-permute-start(f32[1,6,2,64,128]{4,3,2,1,0:T(8,128)S(1)} %get-tuple-element.58), channel_id=1, source_target_pairs={{1,0},{2,1},{3,2},{4,3},{5,4},{6,5},{7,6},{8,7},{9,8},{10,9},{11,1... | collective-permute-start | bytes 1179656 | tf_op jit(solution)/shard_map/ppermute | solution.py:28
  16.2 3.2 slice-start
  16.7 2.8 copy-start
  20.3 7.0 collective-permute-start.2
  24.1 7.0 collective-permute-start.3
  32.7 6.9 copy-start.58
  32.8 6.9 copy-start.56
  32.9 6.8 copy-start.39
  33.4 6.4 copy-start.54
  33.9 5.8 copy-start.52
  34.0 9.1 %collective-permute-start.4 = (f32[1,6,2,64,128]{4,3,2,1,0:T(8,128)S(1)}, f32[1,6,2,64,128]{4,3,2,1,0:T(8,128)S(1)}, u32[]{:S(2)}, u32[]{:S(2)}) collective-permute-start(f32[1,6,2,64,128]{4,3,2,1,0:T(8,128)S(1)} %get-tuple-element.68), channel_id=1, source_target_pairs={{0,1},{1,2},{2,3},{3,4},{4,5},{5,6},{6,7},{7,8},{8,9},{9,10},{10,1... | collective-permute-start | bytes 1179656 | tf_op jit(solution)/shard_map/ppermute | solution.py:27
  35.9 8.9 %collective-permute-start.5 = (f32[1,6,2,64,128]{4,3,2,1,0:T(8,128)S(1)}, f32[1,6,2,64,128]{4,3,2,1,0:T(8,128)S(1)}, u32[]{:S(2)}, u32[]{:S(2)}) collective-permute-start(f32[1,6,2,64,128]{4,3,2,1,0:T(8,128)S(1)} %get-tuple-element.69), channel_id=1, source_target_pairs={{1,0},{2,1},{3,2},{4,3},{5,4},{6,5},{7,6},{8,7},{9,8},{10,9},{11,1... | collective-permute-start | bytes 1179656 | tf_op jit(solution)/shard_map/ppermute | solution.py:28
  45.7 6.6 copy-start.28
  46.6 7.3 %collective-permute-start.6 = (f32[1,3,2,64,128]{4,3,2,1,0:T(8,128)}, f32[1,3,2,64,128]{4,3,2,1,0:T(8,128)}, u32[]{:S(2)}, u32[]{:S(2)}) collective-permute-start(f32[1,3,2,64,128]{4,3,2,1,0:T(8,128)} %get-tuple-element.87), channel_id=1, source_target_pairs={{1,0},{2,1},{3,2},{4,3},{5,4},{6,5},{7,6},{8,7},{9,8},{10,9},{11,1... | collective-permute-start | bytes 589832 | tf_op jit(solution)/shard_map/ppermute | solution.py:28
  50.4 7.3 %collective-permute-start.7 = (f32[1,3,2,64,128]{4,3,2,1,0:T(8,128)}, f32[1,3,2,64,128]{4,3,2,1,0:T(8,128)}, u32[]{:S(2)}, u32[]{:S(2)}) collective-permute-start(f32[1,3,2,64,128]{4,3,2,1,0:T(8,128)} %get-tuple-element.88), channel_id=1, source_target_pairs={{0,1},{1,2},{2,3},{3,4},{4,5},{5,6},{6,7},{7,8},{8,9},{9,10},{10,1... | collective-permute-start | bytes 589832 | tf_op jit(solution)/shard_map/ppermute | solution.py:27
  52.3 11.6 %copy-start.1 = (f32[1,9,8,64,128]{4,3,2,1,0:T(8,128)S(1)}, f32[1,9,8,64,128]{4,3,2,1,0:T(8,128)}, u32[]{:S(2)}) copy-start(f32[1,9,8,64,128]{4,3,2,1,0:T(8,128)} %param.7) | copy-start | bytes 7077892
  63.9 3.9 copy-start.12
  63.9 4.8 copy-start.10
  63.9 4.8 copy-start.33
  64.0 3.0 copy-start.57
  67.8 13.9 %copy-start.37 = (f32[1,1,8,64,128]{4,3,2,1,0:T(8,128)}, f32[1,1,8,64,128]{4,3,2,1,0:T(8,128)S(1)}, u32[]{:S(2)}) copy-start(f32[1,1,8,64,128]{4,3,2,1,0:T(8,128)S(1)} %get-tuple-element.37) | copy-start | bytes 786436
  68.7 8.5 %copy-start.64 = (s32[4]{0:T(128)S(1)}, s32[4]{0:T(128)}, u32[]{:S(2)}) copy-start(s32[4]{0:T(128)} %param.9) | copy-start | bytes 52
  71.6 10.6 %collective-permute-start.8 = (f32[1,6,2,64,128]{4,3,2,1,0:T(8,128)}, f32[1,6,2,64,128]{4,3,2,1,0:T(8,128)}, u32[]{:S(2)}, u32[]{:S(2)}) collective-permute-start(f32[1,6,2,64,128]{4,3,2,1,0:T(8,128)} %get-tuple-element.66), channel_id=1, source_target_pairs={{0,1},{1,2},{2,3},{3,4},{4,5},{5,6},{6,7},{7,8},{8,9},{9,10},{10,1... | collective-permute-start | bytes 1179656 | tf_op jit(solution)/shard_map/ppermute | solution.py:27
  73.5 9.2 %collective-permute-start.9 = (f32[1,6,2,64,128]{4,3,2,1,0:T(8,128)}, f32[1,6,2,64,128]{4,3,2,1,0:T(8,128)}, u32[]{:S(2)}, u32[]{:S(2)}) collective-permute-start(f32[1,6,2,64,128]{4,3,2,1,0:T(8,128)} %get-tuple-element.67), channel_id=1, source_target_pairs={{1,0},{2,1},{3,2},{4,3},{5,4},{6,5},{7,6},{8,7},{9,8},{10,9},{11,1... | collective-permute-start | bytes 1179656 | tf_op jit(solution)/shard_map/ppermute | solution.py:28
  84.5 7.0 copy-start.62
  85.2 8.1 %copy-start.26 = (f32[1,3,8,64,128]{4,3,2,1,0:T(8,128)}, f32[1,3,8,64,128]{4,3,2,1,0:T(8,128)S(1)}, u32[]{:S(2)}) copy-start(f32[1,3,8,64,128]{4,3,2,1,0:T(8,128)S(1)} %fusion.90) | copy-start | bytes 2359300
  86.1 7.5 %collective-permute-start.10 = (f32[1,3,2,64,128]{4,3,2,1,0:T(8,128)}, f32[1,3,2,64,128]{4,3,2,1,0:T(8,128)}, u32[]{:S(2)}, u32[]{:S(2)}) collective-permute-start(f32[1,3,2,64,128]{4,3,2,1,0:T(8,128)} %get-tuple-element.82), channel_id=1, source_target_pairs={{1,0},{2,1},{3,2},{4,3},{5,4},{6,5},{7,6},{8,7},{9,8},{10,9},{11,1... | collective-permute-start | bytes 589832 | tf_op jit(solution)/shard_map/ppermute | solution.py:28
  89.6 7.3 %collective-permute-start.11 = (f32[1,3,2,64,128]{4,3,2,1,0:T(8,128)}, f32[1,3,2,64,128]{4,3,2,1,0:T(8,128)}, u32[]{:S(2)}, u32[]{:S(2)}) collective-permute-start(f32[1,3,2,64,128]{4,3,2,1,0:T(8,128)} %get-tuple-element.83), channel_id=1, source_target_pairs={{0,1},{1,2},{2,3},{3,4},{4,5},{5,6},{6,7},{7,8},{8,9},{9,10},{10,1... | collective-permute-start | bytes 589832 | tf_op jit(solution)/shard_map/ppermute | solution.py:27
  93.3 9.8 %copy-start.60 = (f32[1,1,8,64,128]{4,3,2,1,0:T(8,128)S(1)}, f32[1,1,8,64,128]{4,3,2,1,0:T(8,128)}, u32[]{:S(2)}) copy-start(f32[1,1,8,64,128]{4,3,2,1,0:T(8,128)} %get-tuple-element.43) | copy-start | bytes 786436
  93.3 419.0 %reduce-scatter.5.cloned.1.call-start = ((), (), s32[]{:S(2)}) async-start(), calls=%async_computation.3 | async-start | bytes 278528 | tf_op jit(solution)/shard_map/reduce_scatter | solution.py:132
  103.1 2.5 copy-start.14
  103.1 29.0 %copy-start.18 = (f32[1,3,8,64,128]{4,3,2,1,0:T(8,128)}, f32[1,3,8,64,128]{4,3,2,1,0:T(8,128)S(1)}, u32[]{:S(2)}) copy-start(f32[1,3,8,64,128]{4,3,2,1,0:T(8,128)S(1)} %get-tuple-element.81) | copy-start | bytes 2359300
  104.6 7.4 %copy-start.45 = (f32[1,1,8,64,128]{4,3,2,1,0:T(8,128)}, f32[1,1,8,64,128]{4,3,2,1,0:T(8,128)S(1)}, u32[]{:S(2)}) copy-start(f32[1,1,8,64,128]{4,3,2,1,0:T(8,128)S(1)} %get-tuple-element.27) | copy-start | bytes 786436
  105.6 6.5 copy-start.41
  106.3 5.7 copy-start.43
  106.4 9.1 %collective-permute-start.12 = (f32[1,6,2,64,128]{4,3,2,1,0:T(8,128)S(1)}, f32[1,6,2,64,128]{4,3,2,1,0:T(8,128)S(1)}, u32[]{:S(2)}, u32[]{:S(2)}) collective-permute-start(f32[1,6,2,64,128]{4,3,2,1,0:T(8,128)S(1)} %get-tuple-element.64), channel_id=1, source_target_pairs={{0,1},{1,2},{2,3},{3,4},{4,5},{5,6},{6,7},{7,8},{8,9},{9,10},{10,1... | collective-permute-start | bytes 1179656 | tf_op jit(solution)/shard_map/ppermute | solution.py:27
  108.3 8.9 %collective-permute-start.13 = (f32[1,6,2,64,128]{4,3,2,1,0:T(8,128)S(1)}, f32[1,6,2,64,128]{4,3,2,1,0:T(8,128)S(1)}, u32[]{:S(2)}, u32[]{:S(2)}) collective-permute-start(f32[1,6,2,64,128]{4,3,2,1,0:T(8,128)S(1)} %get-tuple-element.65), channel_id=1, source_target_pairs={{1,0},{2,1},{3,2},{4,3},{5,4},{6,5},{7,6},{8,7},{9,8},{10,9},{11,1... | collective-permute-start | bytes 1179656 | tf_op jit(solution)/shard_map/ppermute | solution.py:28
  112.5 4.8 copy-start.27
  118.9 10.8 %collective-permute-start.14 = (f32[1,3,2,64,128]{4,3,2,1,0:T(8,128)S(1)}, f32[1,3,2,64,128]{4,3,2,1,0:T(8,128)S(1)}, u32[]{:S(2)}, u32[]{:S(2)}) collective-permute-start(f32[1,3,2,64,128]{4,3,2,1,0:T(8,128)S(1)} %get-tuple-element.77), channel_id=1, source_target_pairs={{1,0},{2,1},{3,2},{4,3},{5,4},{6,5},{7,6},{8,7},{9,8},{10,9},{11,1... | collective-permute-start | bytes 589832 | tf_op jit(solution)/shard_map/ppermute | solution.py:28
  122.7 10.3 %copy-start.61 = (f32[1,1,8,64,128]{4,3,2,1,0:T(8,128)S(1)}, f32[1,1,8,64,128]{4,3,2,1,0:T(8,128)}, u32[]{:S(2)}) copy-start(f32[1,1,8,64,128]{4,3,2,1,0:T(8,128)} %get-tuple-element.43) | copy-start | bytes 786436
  122.8 8.0 %collective-permute-start.15 = (f32[1,3,2,64,128]{4,3,2,1,0:T(8,128)S(1)}, f32[1,3,2,64,128]{4,3,2,1,0:T(8,128)S(1)}, u32[]{:S(2)}, u32[]{:S(2)}) collective-permute-start(f32[1,3,2,64,128]{4,3,2,1,0:T(8,128)S(1)} %get-tuple-element.78), channel_id=1, source_target_pairs={{0,1},{1,2},{2,3},{3,4},{4,5},{5,6},{6,7},{7,8},{8,9},{9,10},{10,1... | collective-permute-start | bytes 589832 | tf_op jit(solution)/shard_map/ppermute | solution.py:27
  304.3 7.3 %copy-start.21 = (f32[1,3,8,64,128]{4,3,2,1,0:T(8,128)S(1)}, f32[1,3,8,64,128]{4,3,2,1,0:T(8,128)}, u32[]{:S(2)}) copy-start(f32[1,3,8,64,128]{4,3,2,1,0:T(8,128)} %copy-done.20) | copy-start | bytes 2359300
  304.3 7.3 %copy-start.31 = (f32[1,3,8,64,128]{4,3,2,1,0:T(8,128)S(1)}, f32[1,3,8,64,128]{4,3,2,1,0:T(8,128)}, u32[]{:S(2)}) copy-start(f32[1,3,8,64,128]{4,3,2,1,0:T(8,128)} %copy-done.30) | copy-start | bytes 2359300
  304.3 7.3 %copy-start.34 = (f32[1,3,8,64,128]{4,3,2,1,0:T(8,128)S(1)}, f32[1,3,8,64,128]{4,3,2,1,0:T(8,128)}, u32[]{:S(2)}) copy-start(f32[1,3,8,64,128]{4,3,2,1,0:T(8,128)} %copy-done.33) | copy-start | bytes 2359300
  305.8 5.8 copy-start.22
  305.8 5.9 copy-start.15
  305.8 5.9 copy-start.17
  305.8 5.9 copy-start.19
  307.7 3.9 copy-start.23
  307.7 4.0 copy-start.9
  307.7 4.0 copy-start.11
  307.7 4.0 copy-start.13
  309.6 4.8 copy-start.24
  309.7 2.5 copy-start.7
  315.4 399.1 %reduce-scatter.3.cloned.1.call-start = ((), (), s32[]{:S(2)}) async-start(), calls=%async_computation.2 | async-start | bytes 278528 | tf_op jit(solution)/shard_map/reduce_scatter | solution.py:131
  320.9 2.7 copy-start.32
  320.9 2.7 copy-start.42
  321.8 3.6 copy-start.44
  (24 other events, 35.5 us)
Sparse Core Ops, SparseCore 0:
  93.4 210.8 all-reduce.18
  315.5 196.7 reduce-scatter.4
  516.5 197.9 reduce-scatter.2
where the time goes:
time: 723 us; the launch traced here: 722 us
  waiting for transfers between devices  583 us (81%)
  other arithmetic  54.3 us (8%)
  starting transfers between devices  50.3 us (7%)
  between operations  17.6 us (2%)
  local copies, waits for them, and re-layouts  17 us (2%)
    reduce_scatter x1, waiting for transfers between devices, local(): lax.psum_scatter(kernel_lambda, 'src', scatter_dimension=1, tiled=True)  201 us
    reduce_scatter x1, waiting for transfers between devices, local(): lax.psum_scatter(kernel_mu, 'src', scatter_dimension=1, tiled=True)  185 us
    psum x1, waiting for transfers between devices, spread(): return lax.psum(block, axis)  170 us
    ppermute x8, starting transfers between devices, extended(): after = lax.ppermute(initial, axis, down)  29.5 us
    ppermute x8, starting transfers between devices, extended(): before = lax.ppermute(last, axis, up)  20.5 us
    ppermute x8, waiting for transfers between devices, extended(): before = lax.ppermute(last, axis, up)  18.8 us
    div x4, other arithmetic, diff_valid(): return (8.0 * near - far) / 12.0  14.9 us
  transfers between devices with their start and end apart: 19, of which 16 were waited for; matrix products, arithmetic and copies ran while one was open for 4% of the time, Pallas kernels for 0%

commit v1 on v0

v1 whole, which is shorter than its diff:
```python
import functools

import jax
import jax.numpy as jnp
from jax import lax
from jax.experimental import pallas as pl
from jax.experimental.pallas import tpu as pltpu
from jax.sharding import PartitionSpec as P

STEPS = 4
DT = 0.3
SRC = 16
ZS = 8
NX, NY, NZ = 8, 64, 128
REGIONS = 8
F32 = jnp.float32
BF16 = jnp.bfloat16

WIDE = (0, 4, 5)
FORCE = ((0, 5, 4), (5, 1, 3), (4, 3, 2))

DEPTH = [6, 6, 6] + [8 if comp in WIDE else 6 for comp in range(6)]
EXACT = 2
TOP = {}
for _field in range(9):
    for _d in range(1, DEPTH[_field] + 1):
        TOP[_field, _d] = len(TOP)
REST = {}
for _field in range(9):
    for _d in range(1, EXACT + 1):
        REST[_field, _d] = len(TOP) + len(REST)
MESSAGE = len(TOP) + len(REST)
LABELS = 6

VMEM = pl.BlockSpec(memory_space=pltpu.VMEM)
SMEM = pl.BlockSpec(memory_space=pltpu.SMEM)


def params(mib):
    return pltpu.CompilerParams(vmem_limit_bytes=mib * 2**20)


def shape(*dims, dtype=F32):
    return jax.ShapeDtypeStruct(dims, dtype)


def lookup(region, table):
    value = jnp.full(region.shape, table[0], F32)
    for label in range(1, REGIONS):
        value = jnp.where(region == label, table[label], value)
    return value


def put_row(message, field, d, value):
    top = value.astype(BF16)
    message[TOP[field, d]] = top
    if d <= EXACT:
        message[REST[field, d]] = (value - top.astype(F32)).astype(BF16)


def get_row(message, field, d):
    value = message[TOP[field, d]].astype(F32)
    if d <= EXACT:
        value = value + message[REST[field, d]].astype(F32)
    return value


def put_edges(to_low, to_high, field, x, value, low, high):
    if x < DEPTH[field]:
        put_row(to_low, field, x + 1, value * low)
    if NX - x <= DEPTH[field]:
        put_row(to_high, field, NX - x, value * high)


def pack_kernel(flags, region, state, to_low, to_high):
    low, high = flags[0], flags[1]
    for field in range(9):
        for x in range(NX):
            put_edges(to_low, to_high, field, x, state[field, x], low, high)
    for d in range(1, LABELS + 1):
        to_low[MESSAGE + d - 1] = ((region[d - 1] + 1).astype(F32) * low).astype(BF16)
        to_high[MESSAGE + d - 1] = ((region[NX - d] + 1).astype(F32) * high).astype(BF16)


def bank_kernel(bank, slabs):
    for x in range(NX):
        for comp in range(6):
            for half in range(2):
                slabs[x * 2 + half, comp] = bank[comp, x, half * 32 : half * 32 + 32]


def material_kernel(tables, region, below, above, bu, lam_step, mu_step):
    tab = [[tables[k, i] * (DT / 12.0) for i in range(REGIONS)] for k in range(3)]
    for x in range(-6, NX + 6):
        if 0 <= x < NX:
            label = (region[x] + 1).astype(F32)
        elif x < 0:
            label = below[MESSAGE - x - 1].astype(F32)
        else:
            label = above[MESSAGE + x - NX].astype(F32)
        zero = jnp.zeros((NY, NZ), F32)
        values = [zero, zero, zero]
        for i in range(REGIONS):
            here = label == float(i + 1)
            values = [jnp.where(here, tab[k][i], values[k]) for k in range(3)]
        lam_step[x + 6] = values[0]
        mu_step[x + 6] = values[1]
        bu[x + 6] = values[2]


def shift_y(f, k):
    zero = jnp.zeros((abs(k), f.shape[1]), f.dtype)
    if k > 0:
        return jnp.concatenate([f[k:], zero], 0)
    return jnp.concatenate([zero, f[: f.shape[0] + k]], 0)


def diff_y(f):
    return 8.0 * (shift_y(f, 1) - shift_y(f, -1)) - (shift_y(f, 2) - shift_y(f, -2))


def diff_z(f, band):
    top = f.astype(BF16)
    rest = (f - top.astype(F32)).astype(BF16)
    return jnp.dot(jnp.concatenate([top, rest], 1), band, preferred_element_type=F32)


def double_kernel(last, flags, state, below, above, bu, lam_step, mu_step, band_ref, mid, out, *rest):
    if last:
        v1, s1, v2 = rest
    else:
        to_low, to_high, v1, s1, v2 = rest
        low, high = flags[0], flags[1]
    band = band_ref[...]

    def start(field, x):
        if 0 <= x < NX:
            return state[field, x]
        return get_row(below, field, -x) if x < 0 else get_row(above, field, x - NX + 1)

    def stress0(comp, x):
        return start(3 + comp, x)

    def velocity0(comp, x):
        return start(comp, x)

    def velocity1(comp, x):
        return v1[comp, x + 6]

    def stress1(comp, x):
        if 0 <= x < NX:
            return mid[comp, x]
        return s1[comp, x + 4] if x < 0 else s1[comp, x - NX + 4]

    def velocity2(comp, x):
        if 0 <= x < NX:
            return out[comp, x]
        return v2[comp, x + 2] if x < 0 else v2[comp, 2 + x - NX]

    def diff_x(field, comp, x):
        return 8.0 * (field(comp, x + 1) - field(comp, x - 1)) - (field(comp, x + 2) - field(comp, x - 2))

    def new_velocity(velocity, stress, x):
        b = bu[x + 6]
        for comp, (cx, cy, cz) in enumerate(FORCE):
            force = diff_x(stress, cx, x) + diff_y(stress(cy, x)) + diff_z(stress(cz, x), band)
            yield comp, velocity(comp, x) + b * force

    def new_stress(stress, velocity, x):
        lam, mu = lam_step[x + 6], mu_step[x + 6]
        v = [velocity(comp, x) for comp in range(3)]
        dx = [diff_x(velocity, comp, x) for comp in range(3)]
        dy = [diff_y(v[comp]) for comp in range(3)]
        dz = [diff_z(v[comp], band) for comp in range(3)]
        common = lam * (dx[0] + dy[1] + dz[2])
        twice = mu + mu
        return [
            stress(0, x) + (common + twice * dx[0]),
            stress(1, x) + (common + twice * dy[1]),
            stress(2, x) + (common + twice * dz[2]),
            stress(3, x) + mu * (dz[1] + dy[2]),
            stress(4, x) + mu * (dz[0] + dx[2]),
            stress(5, x) + mu * (dy[0] + dx[1]),
        ]

    for x in range(-6, NX + 6):
        for comp, new in new_velocity(velocity0, stress0, x):
            v1[comp, x + 6] = new
    for x in range(-4, NX + 4):
        for comp, new in enumerate(new_stress(stress0, velocity1, x)):
            if 0 <= x < NX:
                mid[comp, x] = new
            elif x < 0:
                s1[comp, x + 4] = new
            else:
                s1[comp, x - NX + 4] = new
    for x in range(-2, NX + 2):
        for comp, new in new_velocity(velocity1, stress1, x):
            if 0 <= x < NX:
                out[comp, x] = new
                if not last:
                    put_edges(to_low, to_high, comp, x, new, low, high)
            elif x < 0:
                v2[comp, x + 2] = new
            else:
                v2[comp, 2 + x - NX] = new
    for x in range(NX):
        for comp, new in enumerate(new_stress(stress1, velocity2, x)):
            out[3 + comp, x] = new
            if not last:
                put_edges(to_low, to_high, 3 + comp, x, new, low, high)


def correlate_kernel(place, *refs):
    states = refs[:STEPS]
    parts = refs[STEPS : STEPS + ZS]
    out = refs[-1]
    z, half = place[0], place[1]
    lower = lax.broadcasted_iota(jnp.int32, (8, NZ), 0) < 4
    for k in range(ZS):
        x = lax.rem(z + ZS - k, ZS)
        for e in range(2):
            which = half if e == 0 else 1 - half
            y0 = pl.multiple_of(which * 32, 32)
            p = jnp.zeros((32, NZ), F32)
            q = jnp.zeros((32, NZ), F32)
            for t in range(STEPS):
                skip = 3 * (t % 2)
                s = [states[t][skip + comp, x, pl.ds(y0, 32), :] for comp in range(6)]
                r = [parts[k][e, t, comp].astype(F32) for comp in range(6)]
                p = p + (s[0] + s[1] + s[2]) * (r[0] + r[1] + r[2])
                diag = s[0] * r[0] + s[1] * r[1] + s[2] * r[2]
                off = s[3] * r[3] + s[4] * r[4] + s[5] * r[5]
                q = q + diag + (off + off)
            for g in range(4):
                pv, qv = p[g * 8 : g * 8 + 8], q[g * 8 : g * 8 + 8]
                d = which * 8 + g * 2
                out[d, x] = jnp.where(lower, pv, pltpu.roll(qv, 4, 0))
                out[d + 1, x] = jnp.where(lower, pltpu.roll(pv, 4, 0), qv)


def finish_kernel(tables, place, region, terms, k_lambda, k_mu):
    src = place[2]
    tab = [[tables[k, i] for i in range(REGIONS)] for k in range(2)]
    group = pl.multiple_of((src // 2) * 8, 8)
    upper = lax.broadcasted_iota(jnp.int32, (8, NZ), 0) >= 4
    flip = jnp.where(upper, 1, 0) != src % 2
    for x in range(NX):
        total = terms[0, x]
        for s in range(1, SRC):
            total = total + terms[s, x]
        reg = region[x, pl.ds(group, 8), :]
        reg = jnp.where(flip, pltpu.roll(reg, 4, 0), reg)
        lame, shear = lookup(reg, tab[0]), lookup(reg, tab[1])
        theta = total / (3.0 * lame + 2.0 * shear)
        k_lambda[x] = (DT * theta)[:4]
        mu_term = (pltpu.roll(total, 4, 0) - lame * theta) * (DT / shear)
        k_mu[x] = mu_term[:4]


def src_moves(dz, dy):
    moves = []
    for z in range(ZS):
        for y in range(2):
            moves.append((z * 2 + y, ((z + dz) % ZS) * 2 + (y ^ dy)))
    return moves


def gather_receivers(slabs, owners):
    slabs = lax.all_to_all(slabs, "src", 0, 0, tiled=True)
    mine = jnp.stack([lax.dynamic_index_in_dim(slabs, owners[t], 0, keepdims=False) for t in range(STEPS)])
    other = lax.ppermute(mine, "src", src_moves(0, 1))
    pair = jnp.stack([mine, other])
    parts = [pair] + [None] * (ZS - 1)
    up = down = pair
    for k in range(1, 5):
        up = lax.ppermute(up, "src", src_moves(1, 0))
        parts[k] = up
        if k < 4:
            down = lax.ppermute(down, "src", src_moves(-1, 0))
            parts[ZS - k] = down
    return parts


def exchange(to_low, to_high):
    n = lax.axis_size("space")
    below = lax.ppermute(to_high, "space", [(i, (i + 1) % n) for i in range(n)])
    above = lax.ppermute(to_low, "space", [((i + 1) % n, i) for i in range(n)])
    return below, above


def local(wavefield, strain_bank, owners, region, region_lambda, region_mu, region_buoyancy):
    n = lax.axis_size("space")
    pos = lax.axis_index("space")
    src = lax.axis_index("src")
    flags = jnp.stack([(pos > 0).astype(F32), (pos < n - 1).astype(F32)])
    place = jnp.stack([src // 2, src % 2, src]).astype(jnp.int32)
    tables = jnp.stack([region_lambda, region_mu, region_buoyancy])
    eye = functools.partial(jnp.eye, NZ, dtype=F32)
    band = 8.0 * (eye(k=-1) - eye(k=1)) - (eye(k=-2) - eye(k=2))
    band = jnp.concatenate([band, band], 0).astype(BF16)
    state = wavefield[0]

    to_low, to_high = pl.pallas_call(
        pack_kernel,
        out_shape=[shape(MESSAGE + LABELS, NY, NZ, dtype=BF16)] * 2,
        in_specs=[SMEM, VMEM, VMEM],
        out_specs=[VMEM] * 2,
        compiler_params=params(12),
        name="pack",
    )(flags, region, state)
    slabs = pl.pallas_call(
        bank_kernel,
        out_shape=shape(SRC, 6, 32, NZ, dtype=BF16),
        in_specs=[VMEM],
        out_specs=VMEM,
        compiler_params=params(8),
        cost_estimate=pl.CostEstimate(flops=1_000_000, bytes_accessed=40_000_000, transcendentals=0),
        name="bank",
    )(strain_bank[0])
    parts = gather_receivers(slabs, owners)

    states = []
    for pair in range(STEPS // 2):
        below, above = exchange(to_low, to_high)
        if pair == 0:
            bu, lam_step, mu_step = pl.pallas_call(
                material_kernel,
                out_shape=[shape(NX + 12, NY, NZ)] * 3,
                in_specs=[SMEM, VMEM, VMEM, VMEM],
                out_specs=[VMEM] * 3,
                compiler_params=params(12),
                name="material",
            )(tables, region, below, above)
        last = pair == STEPS // 2 - 1
        outs = [shape(6, NX, NY, NZ), shape(9, NX, NY, NZ)]
        outs += [] if last else [shape(MESSAGE, NY, NZ, dtype=BF16)] * 2
        mid, state, *messages = pl.pallas_call(
            functools.partial(double_kernel, last),
            out_shape=outs,
            in_specs=[SMEM] + [VMEM] * 7,
            out_specs=[VMEM] * len(outs),
            scratch_shapes=[
                pltpu.VMEM((3, NX + 12, NY, NZ), F32),
                pltpu.VMEM((6, 8, NY, NZ), F32),
                pltpu.VMEM((3, 4, NY, NZ), F32),
            ],
            compiler_params=params(20),
            cost_estimate=pl.CostEstimate(flops=40_000_000, bytes_accessed=20_000_000, transcendentals=0),
            name="double",
        )(flags, state, below, above, bu, lam_step, mu_step, band)
        if not last:
            to_low, to_high = messages
        states += [mid, state]

    terms = pl.pallas_call(
        correlate_kernel,
        out_shape=shape(SRC, NX, 8, NZ),
        in_specs=[SMEM] + [VMEM] * (STEPS + ZS),
        out_specs=VMEM,
        compiler_params=params(18),
        name="correlate",
    )(place, *states, *parts)

    total = lax.all_to_all(terms, "src", 0, 0, tiled=True)
    kernel_lambda, kernel_mu = pl.pallas_call(
        finish_kernel,
        out_shape=[shape(NX, NY // SRC, NZ)] * 2,
        in_specs=[SMEM, SMEM, VMEM, VMEM],
        out_specs=[VMEM] * 2,
        compiler_params=params(12),
        name="finish",
    )(tables, place, region, total)
    return state[None], kernel_lambda, kernel_mu


def solution(mesh):
    in_specs = (
        P("src", None, "space", None, None),
        P("src", None, "space", None, None),
        P(),
        P("space", None, None),
        P(),
        P(),
        P(),
    )
    out_specs = (
        P("src", None, "space", None, None),
        P("space", "src", None),
        P("space", "src", None),
    )
    return jax.shard_map(local, mesh=mesh, in_specs=in_specs, out_specs=out_specs, check_vma=False)
```

time: 723 us -> 134 us (0.19)
  waiting for transfers between devices: 583 us -> 29.8 us
  other arithmetic: 54.3 us -> 0.39 us
  Pallas kernels: 0 us -> 28.2 us
  blocking collectives: 0 us -> 25.9 us
  starting transfers between devices: 50.3 us -> 27.9 us
  between operations: 17.6 us -> 8.55 us
    reduce_scatter x2 -> x0, waiting for transfers between devices: 386 us -> none  [the longest x1 201 us: local(): lax.psum_scatter(kernel_lambda, 'src', scatter_dimension=1, tiled=True)]
    psum x1 -> x0, waiting for transfers between devices: 170 us -> none  [spread(): return lax.psum(block, axis)]
    ppermute x16 -> x12, starting transfers between devices: 50 us -> 16.6 us  [the longest x3 9.67 us: gather_receivers(): down = lax.ppermute(down, 'src', src_moves(-1, 0))]
    pallas_call x0 -> x7, Pallas kernels: none -> 28.2 us  [the longest x2 18.5 us: local(): pl.pallas_call(functools.partial(double_kernel, last), out_shape=outs, in...]
    all_to_all x0 -> x1, blocking collectives: none -> 25.9 us  [local(): total = lax.all_to_all(terms, 'src', 0, 0, tiled=True)]
    div x4 -> x0, other arithmetic: 14.9 us -> none  [diff_valid(): return (8.0 * near - far) / 12.0]
    unnamed x21 -> x0, other arithmetic: 14.2 us -> none
    all_to_all x0 -> x1, waiting for transfers between devices: none -> 11.9 us  [gather_receivers(): slabs = lax.all_to_all(slabs, 'src', 0, 0, tiled=True)]
  transfers between devices with their start and end apart: 19 -> 13, of which waited for: 16 -> 4; matrix products, arithmetic and copies ran while one was open for 4% -> 1% of each run, Pallas kernels for 0% -> 18%
where the time goes in v1:
time: 134 us; the launch traced here: 133 us
  waiting for transfers between devices  29.8 us (22%)
  Pallas kernels  28.2 us (21%)
  starting transfers between devices  27.9 us (21%)
  blocking collectives  25.9 us (19%)
  local copies, waits for them, and re-layouts  12.3 us (9%)
  between operations  8.55 us (6%)
    all_to_all x1, blocking collectives, local(): total = lax.all_to_all(terms, 'src', 0, 0, tiled=True)  25.9 us
    pallas_call x2, Pallas kernels, local(): pl.pallas_call(functools.partial(double_kernel, last), out_shape=outs, in...  18.5 us
    all_to_all x1, waiting for transfers between devices, gather_receivers(): slabs = lax.all_to_all(slabs, 'src', 0, 0, tiled=True)  11.9 us
    ppermute x3, waiting for transfers between devices, gather_receivers(): down = lax.ppermute(down, 'src', src_moves(-1, 0))  11.5 us
    all_to_all x1, starting transfers between devices, gather_receivers(): slabs = lax.all_to_all(slabs, 'src', 0, 0, tiled=True)  11.4 us
    unnamed x46, local copies, waits for them, and re-layouts  10.8 us
    ppermute x3, starting transfers between devices, gather_receivers(): down = lax.ppermute(down, 'src', src_moves(-1, 0))  9.67 us
    ppermute x1, waiting for transfers between devices, gather_receivers(): other = lax.ppermute(mine, 'src', src_moves(0, 1))  6.43 us
  transfers between devices with their start and end apart: 13, of which 4 were waited for; matrix products, arithmetic and copies ran while one was open for 1% of the time, Pallas kernels for 18%

profile of v1, /device:TPU:2, one launch (start us, length us, event | category | flops | bytes accessed | tf_op | source)
XLA Modules:
  0.0 133.1 jit_solution(18024988464895855625)
XLA Ops:
  0.6 0.0 copy-start.14
  0.6 1.1 copy-done.14
  1.8 0.9 bank.1
  2.7 11.4 %all-to-all-start = ((bf16[16,6,32,128]{3,2,1,0:T(8,128)(2,1)}), bf16[16,6,32,128]{3,2,1,0:T(8,128)(2,1)}, u32[]{:S(2)}, u32[]{:S(2)}) async-start(bf16[16,6,32,128]{3,2,1,0:T(8,128)(2,1)} %bank.1), calls=%async_computation | async-start | bytes 1572864 | tf_op jit(solution)/shard_map/all_to_all | solution.py:270
  14.1 0.0 copy-start.19
  14.1 0.1 add_convert_fusion.flags
  14.2 0.0 copy-done
  14.2 0.0 copy-done.9
  14.2 0.0 copy-start.22
  14.2 2.4 %pack.1 = (bf16[84,64,128]{2,1,0:T(8,128)(2,1)}, bf16[84,64,128]{2,1,0:T(8,128)(2,1)}) custom-call(f32[2]{0:T(128)S(1)} %add_convert_fusion.flags, s32[8,64,128]{2,1,0:T(8,128)S(1)} %copy-done.9, f32[9,8,64,128]{3,2,1,0:T(8,128)S(1)} %bitcast.18), custom_call_target="tpu_custom_call" | custom-call | tf_op jit(solution)/shard_map/pack/pallas_call | solution.py:304
  16.6 0.0 collective-permute-start
  16.6 1.7 %collective-permute-start.1 = (bf16[84,64,128]{2,1,0:T(8,128)(2,1)}, bf16[84,64,128]{2,1,0:T(8,128)(2,1)}, u32[]{:S(2)}, u32[]{:S(2)}) collective-permute-start(bf16[84,64,128]{2,1,0:T(8,128)(2,1)} %get-tuple-element.17), channel_id=1, source_target_pairs={{1,0},{2,1},{3,2},{4,3},{5,4},{6,5},{7,6},{8,7},{9,8},{10,9},{11,1... | collective-permute-start | bytes 4128776 | tf_op jit(solution)/shard_map/ppermute | solution.py:288
  18.4 0.0 copy-done.19
  18.4 0.7 fusion.1
  26.7 11.9 %all-to-all-done = bf16[16,6,32,128]{3,2,1,0:T(8,128)(2,1)} async-done(((bf16[16,6,32,128]{3,2,1,0:T(8,128)(2,1)}), bf16[16,6,32,128]{3,2,1,0:T(8,128)(2,1)}, u32[]{:S(2)}, u32[]{:S(2)}) %all-to-all-start) | async-done | bytes 786464 | tf_op jit(solution)/shard_map/all_to_all | solution.py:270
  38.6 0.9 constant_dynamic-slice_fusion.3
  39.5 0.8 collective-permute-start.4
  40.3 0.0 copy-done.20
  40.3 0.0 copy-done.21
  40.3 0.0 copy-done.22
  40.3 6.4 %collective-permute-done.4 = bf16[4,6,32,128]{3,2,1,0:T(8,128)(2,1)S(1)} collective-permute-done((bf16[4,6,32,128]{3,2,1,0:T(8,128)(2,1)S(1)}, bf16[4,6,32,128]{3,2,1,0:T(8,128)(2,1)S(1)}, u32[]{:S(2)}, u32[]{:S(2)}) %collective-permute-start.4) | collective-permute-done | bytes 196640 | tf_op jit(solution)/shard_map/ppermute | solution.py:272
  46.8 0.0 copy-start.10
  46.8 0.1 collective-permute-start.5
  46.9 0.1 subtract_convert_fusion
  47.1 0.0 collective-permute-done.below
  47.1 0.0 collective-permute-done.1.above
  47.1 2.7 %material.1 = (f32[20,64,128]{2,1,0:T(8,128)S(1)}, f32[20,64,128]{2,1,0:T(8,128)S(1)}, f32[20,64,128]{2,1,0:T(8,128)S(1)}) custom-call(f32[3,8]{1,0:T(4,128)S(1)} %pad_maximum_fusion.3.tables, s32[8,64,128]{2,1,0:T(8,128)S(1)} %copy-done.9, bf16[84,64,128]{2,1,0:T(8,128)(2,1)} %collective-permute-done.below, bf16[84,64,128]{2,1,0:T(8,128)(2,1)} %collective-permute-done.1.above), custom_call_target="tpu_custom_call" | custom-call | tf_op jit(solution)/shard_map/material/pallas_call | solution.py:327
  49.8 0.0 copy-start.4
  49.9 0.0 copy-start.6
  49.9 9.8 %double.2 = (f32[6,8,64,128]{3,2,1,0:T(8,128)S(1)}, f32[9,8,64,128]{3,2,1,0:T(8,128)S(1)}, bf16[78,64,128]{2,1,0:T(8,128)(2,1)}, bf16[78,64,128]{2,1,0:T(8,128)(2,1)}) custom-call(f32[2]{0:T(128)S(1)} %add_convert_fusion.flags, f32[9,8,64,128]{3,2,1,0:T(8,128)S(1)} %bitcast.19, bf16[84,64,128]{2,1,0:T(8,128)(2,1)} %collective-permute-done.below, ...), custom_call_target="tpu_custom_call" | custom-call | flops 40000000 | bytes 20000000 | tf_op jit(solution)/shard_map/double/pallas_call | solution.py:338
  59.6 0.0 copy-done.4
  59.6 0.0 copy-done.6
  59.6 1.4 %copy-done.1 = f32[9,8,64,128]{3,2,1,0:T(8,128)} copy-done((f32[9,8,64,128]{3,2,1,0:T(8,128)}, f32[9,8,64,128]{3,2,1,0:T(8,128)S(1)}, u32[]{:S(2)}) %copy-start.1) | copy-done | bytes 2359320
  61.1 1.1 copy-done.12
  62.2 0.0 collective-permute-start.2
  62.2 4.1 %collective-permute-start.3 = (bf16[78,64,128]{2,1,0:T(8,128)(2,1)}, bf16[78,64,128]{2,1,0:T(8,128)(2,1)}, u32[]{:S(2)}, u32[]{:S(2)}) collective-permute-start(bf16[78,64,128]{2,1,0:T(8,128)(2,1)} %get-tuple-element.23), channel_id=1, source_target_pairs={{1,0},{2,1},{3,2},{4,3},{5,4},{6,5},{7,6},{8,7},{9,8},{10,9},{11,1... | collective-permute-start | bytes 3833864 | tf_op jit(solution)/shard_map/ppermute | solution.py:288
  66.3 2.2 %collective-permute-start.9 = (bf16[2,4,6,32,128]{4,3,2,1,0:T(8,128)(2,1)S(1)}, bf16[2,4,6,32,128]{4,3,2,1,0:T(8,128)(2,1)S(1)}, u32[]{:S(2)}, u32[]{:S(2)}) collective-permute-start(bf16[2,4,6,32,128]{4,3,2,1,0:T(8,128)(2,1)S(1)} %pad_maximum_fusion.refs_4_), channel_id=1, source_target_pairs={{0,224},{16,240},{32,0},{48,16},{64,32},{80,48},{96,64},{112,80},{... | collective-permute-start | bytes 1179656 | tf_op jit(solution)/shard_map/ppermute | solution.py:280
  68.5 0.0 collective-permute-done.5.refs_5_
  68.5 0.1 collective-permute-start.6
  68.6 0.8 copy-done.15
  69.4 6.2 %collective-permute-done.9.refs_11_ = bf16[2,4,6,32,128]{4,3,2,1,0:T(8,128)(2,1)S(1)} collective-permute-done((bf16[2,4,6,32,128]{4,3,2,1,0:T(8,128)(2,1)S(1)}, bf16[2,4,6,32,128]{4,3,2,1,0:T(8,128)(2,1)S(1)}, u32[]{:S(2)}, u32[]{:S(2)}) %collective-permute-start.9) | collective-permute-done | bytes 393248 | tf_op jit(solution)/shard_map/ppermute | solution.py:280
  75.6 3.7 %collective-permute-start.10 = (bf16[2,4,6,32,128]{4,3,2,1,0:T(8,128)(2,1)S(1)}, bf16[2,4,6,32,128]{4,3,2,1,0:T(8,128)(2,1)}, u32[]{:S(2)}, u32[]{:S(2)}) collective-permute-start(bf16[2,4,6,32,128]{4,3,2,1,0:T(8,128)(2,1)S(1)} %collective-permute-done.9.refs_11_), channel_id=1, source_target_pairs={{0,224},{16,240},{32,0},{48,16},{64,32},{80,48},{96,64},{112,80},{... | collective-permute-start | bytes 1179656 | tf_op jit(solution)/shard_map/ppermute | solution.py:280
  79.3 0.0 collective-permute-done.6.refs_6_
  79.3 0.0 collective-permute-start.7
  79.3 0.8 copy-done.17
  80.0 5.4 %collective-permute-done.10.refs_10_ = bf16[2,4,6,32,128]{4,3,2,1,0:T(8,128)(2,1)} collective-permute-done((bf16[2,4,6,32,128]{4,3,2,1,0:T(8,128)(2,1)S(1)}, bf16[2,4,6,32,128]{4,3,2,1,0:T(8,128)(2,1)}, u32[]{:S(2)}, u32[]{:S(2)}) %collective-permute-start.10) | collective-permute-done | bytes 393248 | tf_op jit(solution)/shard_map/ppermute | solution.py:280
  85.4 3.8 %collective-permute-start.11 = (bf16[2,4,6,32,128]{4,3,2,1,0:T(8,128)(2,1)}, bf16[2,4,6,32,128]{4,3,2,1,0:T(8,128)(2,1)}, u32[]{:S(2)}, u32[]{:S(2)}) collective-permute-start(bf16[2,4,6,32,128]{4,3,2,1,0:T(8,128)(2,1)} %collective-permute-done.10.refs_10_), channel_id=1, source_target_pairs={{0,224},{16,240},{32,0},{48,16},{64,32},{80,48},{96,64},{112,80},{... | collective-permute-start | bytes 1179656 | tf_op jit(solution)/shard_map/ppermute | solution.py:280
  89.2 0.0 collective-permute-done.7.refs_7_
  89.2 0.0 collective-permute-start.8
  89.2 0.1 pad_add_fusion.place
  89.3 0.0 collective-permute-done.2.below
  89.3 0.0 collective-permute-done.3.above
  89.3 1.7 %copy-done.2 = f32[9,8,64,128]{3,2,1,0:T(8,128)S(1)} copy-done((f32[9,8,64,128]{3,2,1,0:T(8,128)S(1)}, f32[9,8,64,128]{3,2,1,0:T(8,128)}, u32[]{:S(2)}) %copy-start.2) | copy-done | bytes 2359320
  91.0 1.1 copy-done.5
  92.1 1.1 copy-done.7
  93.2 8.7 %double.3 = (f32[6,8,64,128]{3,2,1,0:T(8,128)S(1)}, f32[9,8,64,128]{3,2,1,0:T(8,128)}) custom-call(f32[2]{0:T(128)S(1)} %add_convert_fusion.flags, f32[9,8,64,128]{3,2,1,0:T(8,128)S(1)} %copy-done.2, bf16[78,64,128]{2,1,0:T(8,128)(2,1)S(1)} %collective-permute-done.2.below, bf16[78,64,128]{2,1,0:T(8,128)(2,1)} %collective-permute-done.3.above, ...), custom_call_target="tpu_custom_call" | custom-call | flops 40000000 | bytes 20000000 | tf_op jit(solution)/shard_map/double/pallas_call | solution.py:338
  101.9 0.0 collective-permute-done.11.refs_9_
  101.9 0.0 collective-permute-done.8.refs_8_
  101.9 0.0 copy-done.3
  102.0 0.0 copy-start.8
  102.0 1.7 %copy-done.8 = f32[9,8,64,128]{3,2,1,0:T(8,128)S(1)} copy-done((f32[9,8,64,128]{3,2,1,0:T(8,128)S(1)}, f32[9,8,64,128]{3,2,1,0:T(8,128)}, u32[]{:S(2)}) %copy-start.8) | copy-done | bytes 2359320
  103.6 2.4 %correlate.1 = f32[16,8,8,128]{3,2,1,0:T(8,128)S(1)} custom-call(s32[3]{0:T(128)S(1)} %pad_add_fusion.place, f32[6,8,64,128]{3,2,1,0:T(8,128)S(1)} %copy-done.13, f32[9,8,64,128]{3,2,1,0:T(8,128)S(1)} %copy-done.3, f32[6,8,64,128]{3,2,1,0:T(8,128)S(1)} %get-tuple-element.26.refs_2_, f32[9,8,64,128]{3,2,1,0:T(8,128)S(1)} %copy-done.8, ...), custom_call_target="tpu_custom_call" | custom-call | tf_op jit(solution)/shard_map/correlate/pallas_call | solution.py:356
  106.0 25.9 %all_to_all.10.terms = f32[16,8,8,128]{3,2,1,0:T(8,128)S(1)} all-to-all(f32[16,8,8,128]{3,2,1,0:T(8,128)S(1)} %correlate.1), channel_id=1, replica_groups=mesh['src'=16,'space'=16] {'src'}, dimensions={0} | all-to-all | bytes 1048576 | tf_op jit(solution)/shard_map/all_to_all | solution.py:365
  131.9 1.2 finish.1
  (27 shorter events, 0.1 us)
Async XLA Ops:
  0.6 1.1 copy-start.14
  1.8 12.4 %copy-start = (f32[1,9,8,64,128]{4,3,2,1,0:T(8,128)S(1)}, f32[1,9,8,64,128]{4,3,2,1,0:T(8,128)}, u32[]{:S(2)}) copy-start(f32[1,9,8,64,128]{4,3,2,1,0:T(8,128)} %param.7) | copy-start | bytes 7077892
  1.8 12.4 %copy-start.9 = (s32[8,64,128]{2,1,0:T(8,128)S(1)}, s32[8,64,128]{2,1,0:T(8,128)}, u32[]{:S(2)}) copy-start(s32[8,64,128]{2,1,0:T(8,128)} %region.5) | copy-start | bytes 786436
  2.7 35.9 %all-to-all-start = ((bf16[16,6,32,128]{3,2,1,0:T(8,128)(2,1)}), bf16[16,6,32,128]{3,2,1,0:T(8,128)(2,1)}, u32[]{:S(2)}, u32[]{:S(2)}) async-start(bf16[16,6,32,128]{3,2,1,0:T(8,128)(2,1)} %bank.1), calls=%async_computation | async-start | bytes 1572864 | tf_op jit(solution)/shard_map/all_to_all | solution.py:270
  14.1 4.3 %copy-start.19 = (s32[4]{0:T(128)S(1)}, s32[4]{0:T(128)}, u32[]{:S(2)}) copy-start(s32[4]{0:T(128)} %param.9) | copy-start | bytes 52
  14.2 26.1 %copy-start.20 = (f32[8]{0:T(128)S(1)}, f32[8]{0:T(128)}, u32[]{:S(2)}) copy-start(f32[8]{0:T(128)} %param.13) | copy-start | bytes 100
  14.2 26.1 %copy-start.21 = (f32[8]{0:T(128)S(1)}, f32[8]{0:T(128)}, u32[]{:S(2)}) copy-start(f32[8]{0:T(128)} %param.12) | copy-start | bytes 100
  14.2 26.1 %copy-start.22 = (f32[8]{0:T(128)S(1)}, f32[8]{0:T(128)}, u32[]{:S(2)}) copy-start(f32[8]{0:T(128)} %param.11) | copy-start | bytes 100
  16.6 30.4 %collective-permute-start = (bf16[84,64,128]{2,1,0:T(8,128)(2,1)}, bf16[84,64,128]{2,1,0:T(8,128)(2,1)}, u32[]{:S(2)}, u32[]{:S(2)}) collective-permute-start(bf16[84,64,128]{2,1,0:T(8,128)(2,1)} %get-tuple-element.16), channel_id=1, source_target_pairs={{0,1},{1,2},{2,3},{3,4},{4,5},{5,6},{6,7},{7,8},{8,9},{9,10},{10,1... | collective-permute-start | bytes 4128776 | tf_op jit(solution)/shard_map/ppermute | solution.py:287
  16.6 30.4 %collective-permute-start.1 = (bf16[84,64,128]{2,1,0:T(8,128)(2,1)}, bf16[84,64,128]{2,1,0:T(8,128)(2,1)}, u32[]{:S(2)}, u32[]{:S(2)}) collective-permute-start(bf16[84,64,128]{2,1,0:T(8,128)(2,1)} %get-tuple-element.17), channel_id=1, source_target_pairs={{1,0},{2,1},{3,2},{4,3},{5,4},{6,5},{7,6},{8,7},{9,8},{10,9},{11,1... | collective-permute-start | bytes 4128776 | tf_op jit(solution)/shard_map/ppermute | solution.py:288
  39.5 7.3 %collective-permute-start.4 = (bf16[4,6,32,128]{3,2,1,0:T(8,128)(2,1)S(1)}, bf16[4,6,32,128]{3,2,1,0:T(8,128)(2,1)S(1)}, u32[]{:S(2)}, u32[]{:S(2)}) collective-permute-start(bf16[4,6,32,128]{3,2,1,0:T(8,128)(2,1)S(1)} %get-tuple-element.34), channel_id=1, source_target_pairs={{0,16},{16,0},{32,48},{48,32},{64,80},{80,64},{96,112},{112,96},{1... | collective-permute-start | bytes 589832 | tf_op jit(solution)/shard_map/ppermute | solution.py:272
  46.8 19.5 %copy-start.10 = (bf16[2,4,6,32,128]{4,3,2,1,0:T(8,128)(2,1)}, bf16[2,4,6,32,128]{4,3,2,1,0:T(8,128)(2,1)S(1)}, u32[]{:S(2)}) copy-start(bf16[2,4,6,32,128]{4,3,2,1,0:T(8,128)(2,1)S(1)} %pad_maximum_fusion.refs_4_) | copy-start | bytes 1179652
  46.8 21.7 %collective-permute-start.5 = (bf16[2,4,6,32,128]{4,3,2,1,0:T(8,128)(2,1)S(1)}, bf16[2,4,6,32,128]{4,3,2,1,0:T(8,128)(2,1)S(1)}, u32[]{:S(2)}, u32[]{:S(2)}) collective-permute-start(bf16[2,4,6,32,128]{4,3,2,1,0:T(8,128)(2,1)S(1)} %pad_maximum_fusion.refs_4_), channel_id=1, source_target_pairs={{0,32},{16,48},{32,64},{48,80},{64,96},{80,112},{96,128},{112,144}... | collective-permute-start | bytes 1179656 | tf_op jit(solution)/shard_map/ppermute | solution.py:277
  49.8 9.8 %copy-start.4 = (f32[20,64,128]{2,1,0:T(8,128)}, f32[20,64,128]{2,1,0:T(8,128)S(1)}, u32[]{:S(2)}) copy-start(f32[20,64,128]{2,1,0:T(8,128)S(1)} %get-tuple-element.19.lam_step) | copy-start | bytes 1966084
  49.9 9.8 %copy-start.6 = (f32[20,64,128]{2,1,0:T(8,128)}, f32[20,64,128]{2,1,0:T(8,128)S(1)}, u32[]{:S(2)}) copy-start(f32[20,64,128]{2,1,0:T(8,128)S(1)} %get-tuple-element.20.mu_step) | copy-start | bytes 1966084
  59.6 1.4 %copy-start.1 = (f32[9,8,64,128]{3,2,1,0:T(8,128)}, f32[9,8,64,128]{3,2,1,0:T(8,128)S(1)}, u32[]{:S(2)}) copy-start(f32[9,8,64,128]{3,2,1,0:T(8,128)S(1)} %get-tuple-element.21.state.refs_1_) | copy-start | bytes 7077892
  61.1 1.1 copy-start.12
  62.2 27.1 %collective-permute-start.2 = (bf16[78,64,128]{2,1,0:T(8,128)(2,1)}, bf16[78,64,128]{2,1,0:T(8,128)(2,1)S(1)}, u32[]{:S(2)}, u32[]{:S(2)}) collective-permute-start(bf16[78,64,128]{2,1,0:T(8,128)(2,1)} %get-tuple-element.22), channel_id=1, source_target_pairs={{0,1},{1,2},{2,3},{3,4},{4,5},{5,6},{6,7},{7,8},{8,9},{9,10},{10,1... | collective-permute-start | bytes 3833864 | tf_op jit(solution)/shard_map/ppermute | solution.py:287
  62.2 27.1 %collective-permute-start.3 = (bf16[78,64,128]{2,1,0:T(8,128)(2,1)}, bf16[78,64,128]{2,1,0:T(8,128)(2,1)}, u32[]{:S(2)}, u32[]{:S(2)}) collective-permute-start(bf16[78,64,128]{2,1,0:T(8,128)(2,1)} %get-tuple-element.23), channel_id=1, source_target_pairs={{1,0},{2,1},{3,2},{4,3},{5,4},{6,5},{7,6},{8,7},{9,8},{10,9},{11,1... | collective-permute-start | bytes 3833864 | tf_op jit(solution)/shard_map/ppermute | solution.py:288
  66.3 9.2 %collective-permute-start.9 = (bf16[2,4,6,32,128]{4,3,2,1,0:T(8,128)(2,1)S(1)}, bf16[2,4,6,32,128]{4,3,2,1,0:T(8,128)(2,1)S(1)}, u32[]{:S(2)}, u32[]{:S(2)}) collective-permute-start(bf16[2,4,6,32,128]{4,3,2,1,0:T(8,128)(2,1)S(1)} %pad_maximum_fusion.refs_4_), channel_id=1, source_target_pairs={{0,224},{16,240},{32,0},{48,16},{64,32},{80,48},{96,64},{112,80},{... | collective-permute-start | bytes 1179656 | tf_op jit(solution)/shard_map/ppermute | solution.py:280
  68.5 10.8 %collective-permute-start.6 = (bf16[2,4,6,32,128]{4,3,2,1,0:T(8,128)(2,1)S(1)}, bf16[2,4,6,32,128]{4,3,2,1,0:T(8,128)(2,1)S(1)}, u32[]{:S(2)}, u32[]{:S(2)}) collective-permute-start(bf16[2,4,6,32,128]{4,3,2,1,0:T(8,128)(2,1)S(1)} %collective-permute-done.5.refs_5_), channel_id=1, source_target_pairs={{0,32},{16,48},{32,64},{48,80},{64,96},{80,112},{96,128},{112,144}... | collective-permute-start | bytes 1179656 | tf_op jit(solution)/shard_map/ppermute | solution.py:277
  68.6 0.8 copy-start.15
  75.6 9.8 %collective-permute-start.10 = (bf16[2,4,6,32,128]{4,3,2,1,0:T(8,128)(2,1)S(1)}, bf16[2,4,6,32,128]{4,3,2,1,0:T(8,128)(2,1)}, u32[]{:S(2)}, u32[]{:S(2)}) collective-permute-start(bf16[2,4,6,32,128]{4,3,2,1,0:T(8,128)(2,1)S(1)} %collective-permute-done.9.refs_11_), channel_id=1, source_target_pairs={{0,224},{16,240},{32,0},{48,16},{64,32},{80,48},{96,64},{112,80},{... | collective-permute-start | bytes 1179656 | tf_op jit(solution)/shard_map/ppermute | solution.py:280
  79.3 9.9 %collective-permute-start.7 = (bf16[2,4,6,32,128]{4,3,2,1,0:T(8,128)(2,1)S(1)}, bf16[2,4,6,32,128]{4,3,2,1,0:T(8,128)(2,1)}, u32[]{:S(2)}, u32[]{:S(2)}) collective-permute-start(bf16[2,4,6,32,128]{4,3,2,1,0:T(8,128)(2,1)S(1)} %collective-permute-done.6.refs_6_), channel_id=1, source_target_pairs={{0,32},{16,48},{32,64},{48,80},{64,96},{80,112},{96,128},{112,144}... | collective-permute-start | bytes 1179656 | tf_op jit(solution)/shard_map/ppermute | solution.py:277
  79.3 0.8 copy-start.17
  85.4 16.5 %collective-permute-start.11 = (bf16[2,4,6,32,128]{4,3,2,1,0:T(8,128)(2,1)}, bf16[2,4,6,32,128]{4,3,2,1,0:T(8,128)(2,1)}, u32[]{:S(2)}, u32[]{:S(2)}) collective-permute-start(bf16[2,4,6,32,128]{4,3,2,1,0:T(8,128)(2,1)} %collective-permute-done.10.refs_10_), channel_id=1, source_target_pairs={{0,224},{16,240},{32,0},{48,16},{64,32},{80,48},{96,64},{112,80},{... | collective-permute-start | bytes 1179656 | tf_op jit(solution)/shard_map/ppermute | solution.py:280
  89.2 12.7 %collective-permute-start.8 = (bf16[2,4,6,32,128]{4,3,2,1,0:T(8,128)(2,1)}, bf16[2,4,6,32,128]{4,3,2,1,0:T(8,128)(2,1)}, u32[]{:S(2)}, u32[]{:S(2)}) collective-permute-start(bf16[2,4,6,32,128]{4,3,2,1,0:T(8,128)(2,1)} %collective-permute-done.7.refs_7_), channel_id=1, source_target_pairs={{0,32},{16,48},{32,64},{48,80},{64,96},{80,112},{96,128},{112,144}... | collective-permute-start | bytes 1179656 | tf_op jit(solution)/shard_map/ppermute | solution.py:277
  89.3 1.7 %copy-start.2 = (f32[9,8,64,128]{3,2,1,0:T(8,128)S(1)}, f32[9,8,64,128]{3,2,1,0:T(8,128)}, u32[]{:S(2)}) copy-start(f32[9,8,64,128]{3,2,1,0:T(8,128)} %copy-done.1) | copy-start | bytes 7077892
  91.0 1.1 copy-start.5
  92.0 1.1 copy-start.7
  93.1 8.8 %copy-start.3 = (f32[9,8,64,128]{3,2,1,0:T(8,128)S(1)}, f32[9,8,64,128]{3,2,1,0:T(8,128)}, u32[]{:S(2)}) copy-start(f32[9,8,64,128]{3,2,1,0:T(8,128)} %copy-done.1) | copy-start | bytes 7077892
  93.1 8.8 %copy-start.11 = (bf16[2,4,6,32,128]{4,3,2,1,0:T(8,128)(2,1)S(1)}, bf16[2,4,6,32,128]{4,3,2,1,0:T(8,128)(2,1)}, u32[]{:S(2)}) copy-start(bf16[2,4,6,32,128]{4,3,2,1,0:T(8,128)(2,1)} %copy-done.10) | copy-start | bytes 1179652
  93.1 8.8 %copy-start.13 = (f32[6,8,64,128]{3,2,1,0:T(8,128)S(1)}, f32[6,8,64,128]{3,2,1,0:T(8,128)}, u32[]{:S(2)}) copy-start(f32[6,8,64,128]{3,2,1,0:T(8,128)} %copy-done.12) | copy-start | bytes 4718596
  93.1 8.8 %copy-start.16 = (bf16[2,4,6,32,128]{4,3,2,1,0:T(8,128)(2,1)S(1)}, bf16[2,4,6,32,128]{4,3,2,1,0:T(8,128)(2,1)}, u32[]{:S(2)}) copy-start(bf16[2,4,6,32,128]{4,3,2,1,0:T(8,128)(2,1)} %copy-done.15) | copy-start | bytes 1179652
  93.1 8.8 %copy-start.18 = (bf16[2,4,6,32,128]{4,3,2,1,0:T(8,128)(2,1)S(1)}, bf16[2,4,6,32,128]{4,3,2,1,0:T(8,128)(2,1)}, u32[]{:S(2)}) copy-start(bf16[2,4,6,32,128]{4,3,2,1,0:T(8,128)(2,1)} %copy-done.17) | copy-start | bytes 1179652
  102.0 1.7 %copy-start.8 = (f32[9,8,64,128]{3,2,1,0:T(8,128)S(1)}, f32[9,8,64,128]{3,2,1,0:T(8,128)}, u32[]{:S(2)}) copy-start(f32[9,8,64,128]{3,2,1,0:T(8,128)} %get-tuple-element.24.refs_3_) | copy-start | bytes 7077892
